TPU v7x, 256 devices: a whole 4x4x8 slice. The times are simulated.
256 devices in a mesh: ctx: 4 (over x), exp: 64 (over z, y, core).
Axes of the slice: x: 4, y: 4, z: 8, core: 2. Of those that a mesh axis runs over, the one named last changes fastest.
Arguments:
- moe_input: bfloat16 [8192, 3584], P('exp', 'ctx'), may hold values from -6 to 6
- moe_grad: bfloat16 [8192, 3584], P('exp', 'ctx'), may hold values from -6 to 6
- routes: int32 [8192, 8], P('exp'), may hold values from 0 to 127, all different within a row; in each aligned block of 128 rows (0 to 127, 128 to 255, ...) at most 10 rows name the same one
- gates: float32 [8192, 8], P('exp'), may hold values from 0.05 to 0.5
- w_gate: bfloat16 [128, 3584, 1024], P('exp', 'ctx'), may hold values from -0.09375 to 0.09375
- w_up: bfloat16 [128, 3584, 1024], P('exp', 'ctx'), may hold values from -0.09375 to 0.09375
- w_down: bfloat16 [128, 1024, 3584], P('exp', None, 'ctx'), may hold values from -0.1875 to 0.1875
- queries: bfloat16 [512, 73728], P('ctx', 'exp'), may hold values from -16 to 16
- out_grad: bfloat16 [512, 65536], P('ctx', 'exp'), may hold values from -6 to 6
- positions: int32 [512], P('ctx'), may hold values from 0 to 1023, as said below
- latents: bfloat16 [1024, 576], P('ctx'), may hold values from -6 to 6
Outputs:
- moe_input_grad: bfloat16 [8192, 3584], P('exp', 'ctx')
- query_grad: bfloat16 [512, 73728], P('ctx', 'exp')
- latent_grad: float32 [1024, 576], P(('ctx', 'exp'))
Inputs may be any that keep to these rules, and one draw needn't show every extreme that they name: `routes`: each row names 8 different experts; among the 128 rows of one index of exp no expert is named more than 10 times, and in some such block one is named exactly 10 times. Row i lies within the keys of its own context shard, (i // 128) * 256 <= positions[i] < (i // 128 + 1) * 256; the first row of each shard sits at the shard's first key and the last row at its last key.
All inputs are finite; a program needn't handle non-finite values.
Results may differ from a plain program's by a relative error of at most 0.018.
Values may be sent and summed in bfloat16 or wider, within the bound.
A program may use at most 128 MiB of HBM per device.

v0:
```python
import jax
import jax.numpy as jnp
from jax import lax
from jax.sharding import PartitionSpec as P

SCORE_SCALE = 192.0 ** (-0.5)
MASKED = -1e30


def swiglu_back(gate_pre, up_pre, hidden_grad):
    sigma = jax.nn.sigmoid(gate_pre)
    gate_back = hidden_grad * up_pre * sigma * (1.0 + gate_pre * (1.0 - sigma))
    up_back = hidden_grad * gate_pre * sigma
    return (gate_back.astype(jnp.bfloat16), up_back.astype(jnp.bfloat16))


def expert_layer(moe_input, moe_grad, routes, gates, w_gate, w_up, w_down):
    tok_rows, width_part = moe_input.shape
    fanout = routes.shape[1]
    local_experts = w_gate.shape[0]
    exp_count = lax.axis_size("exp")
    experts = local_experts * exp_count
    capacity = tok_rows * fanout // experts * 5 // 4
    flat_routes = routes.reshape(-1)
    onehot = (flat_routes[:, None] == jnp.arange(experts, dtype=jnp.int32)[None, :]).astype(
        jnp.int32
    )
    before = jnp.cumsum(onehot, axis=0) - onehot
    slot_index = jnp.sum(before * onehot, axis=1)
    target = flat_routes * capacity + slot_index
    source_rows = jnp.arange(tok_rows * fanout, dtype=jnp.int32) // fanout
    empty = jnp.zeros((experts * capacity, width_part), jnp.bfloat16)
    send_shape = (exp_count, local_experts * capacity, width_part)
    send_input = empty.at[target].set(moe_input[source_rows]).reshape(send_shape)
    send_grad = empty.at[target].set(moe_grad[source_rows]).reshape(send_shape)
    recv_input, recv_grad = (
        lax.all_to_all(send_input, "exp", split_axis=0, concat_axis=0, tiled=True),
        lax.all_to_all(send_grad, "exp", split_axis=0, concat_axis=0, tiled=True),
    )
    slot_shape = (exp_count, local_experts, capacity, width_part)
    recv_input = recv_input.reshape(slot_shape)
    recv_grad = recv_grad.reshape(slot_shape)
    gate_part = jnp.einsum("sekd,edh->sekh", recv_input, w_gate, preferred_element_type=jnp.float32)
    up_part = jnp.einsum("sekd,edh->sekh", recv_input, w_up, preferred_element_type=jnp.float32)
    down_part = jnp.einsum("sekd,ehd->sekh", recv_grad, w_down, preferred_element_type=jnp.float32)
    gate_pre, up_pre, hidden_grad = (
        lax.psum(gate_part.astype(jnp.bfloat16), "ctx").astype(jnp.float32),
        lax.psum(up_part.astype(jnp.bfloat16), "ctx").astype(jnp.float32),
        lax.psum(down_part.astype(jnp.bfloat16), "ctx").astype(jnp.float32),
    )
    gate_back, up_back = swiglu_back(gate_pre, up_pre, hidden_grad)
    route_part = jnp.einsum("sekh,edh->sekd", gate_back, w_gate, preferred_element_type=jnp.float32)
    route_part = route_part + jnp.einsum(
        "sekh,edh->sekd", up_back, w_up, preferred_element_type=jnp.float32
    )
    route_part = route_part.astype(jnp.bfloat16).reshape(send_shape)
    returned = lax.all_to_all(route_part, "exp", split_axis=0, concat_axis=0, tiled=True).reshape(
        experts * capacity, width_part
    )
    per_route = returned[target].reshape(tok_rows, fanout, width_part).astype(jnp.float32)
    return jnp.sum(per_route * gates[:, :, None], axis=1).astype(jnp.bfloat16)


def attention_layer(queries, out_grad, positions, latents):
    q_rows = queries.shape[0]
    lat_width = latents.shape[1]
    head_count = queries.shape[1] // lat_width
    val_width = out_grad.shape[1] // head_count
    query_heads = queries.reshape(q_rows, head_count, lat_width)
    grad_heads = out_grad.reshape(q_rows, head_count, val_width)
    gathered = lax.all_gather(latents, "ctx", axis=0, tiled=True)
    key_count = gathered.shape[0]
    visible = (jnp.arange(key_count, dtype=jnp.int32)[None, :] <= positions[:, None])[None]
    scores = (
        jnp.einsum("qhc,kc->hqk", query_heads, gathered, preferred_element_type=jnp.float32)
        * SCORE_SCALE
    )
    scores = jnp.where(visible, scores, MASKED)
    peak = jnp.max(scores, axis=2, keepdims=True)
    raw = jnp.where(visible, jnp.exp(scores - peak), 0.0)
    attend = raw / jnp.sum(raw, axis=2, keepdims=True)
    value_dot = jnp.einsum(
        "qhv,kv->hqk", grad_heads, gathered[:, :val_width], preferred_element_type=jnp.float32
    )
    row_dot = jnp.sum(attend * value_dot, axis=2, keepdims=True)
    score_grad = (attend * (value_dot - row_dot)).astype(jnp.bfloat16)
    query_grad = (
        jnp.einsum("hqk,kc->qhc", score_grad, gathered, preferred_element_type=jnp.float32)
        * SCORE_SCALE
    )
    key_grad = (
        jnp.einsum("hqk,qhc->kc", score_grad, query_heads, preferred_element_type=jnp.float32)
        * SCORE_SCALE
    )
    value_grad = jnp.einsum(
        "hqk,qhv->kv", attend.astype(jnp.bfloat16), grad_heads, preferred_element_type=jnp.float32
    )
    latent_part = key_grad + jnp.pad(value_grad, ((0, 0), (0, lat_width - val_width)))
    latent_grad = lax.psum_scatter(latent_part, ("ctx", "exp"), scatter_dimension=0, tiled=True)
    query_out = query_grad.astype(jnp.bfloat16).reshape(q_rows, head_count * lat_width)
    return (query_out, latent_grad)


def per_device(
    moe_input, moe_grad, routes, gates, w_gate, w_up, w_down, queries, out_grad, positions, latents
):
    input_grad = expert_layer(moe_input, moe_grad, routes, gates, w_gate, w_up, w_down)
    query_out, latent_grad = attention_layer(queries, out_grad, positions, latents)
    return (input_grad, query_out, latent_grad)


def solution(mesh):
    return jax.shard_map(
        per_device,
        mesh=mesh,
        in_specs=(
            P("exp", "ctx"),
            P("exp", "ctx"),
            P("exp", None),
            P("exp", None),
            P("exp", "ctx", None),
            P("exp", "ctx", None),
            P("exp", None, "ctx"),
            P("ctx", "exp"),
            P("ctx", "exp"),
            P("ctx"),
            P("ctx", None),
        ),
        out_specs=(P("exp", "ctx"), P("ctx", "exp"), P(("ctx", "exp"), None)),
        check_vma=False,
    )
```

profile of v0, /device:TPU:4, one launch (start us, length us, event | category | flops | bytes accessed | tf_op | source)
XLA Modules:
  0.0 668.3 jit_solution(574986967810144389)
XLA Ops:
  10.0 12.8 %scatter_custom_fusion.1 = bf16[1280,896]{1,0:T(8,128)(2,1)S(1)} fusion(s32[1024]{0:T(1024)S(1)} %bitcast.104, bf16[128,896]{1,0:T(8,128)(2,1)S(1)} %copy-done, s32[1024]{0:T(1024)S(1)} %broadcast_clamp_fusion.1, bf16[]{:T(256)} %constant.14.clone.1), kind=kCustom, calls=%fused_computation.37 | custom fusion | bytes 2293762 | tf_op jit(solution)/shard_map/scatter | solution.py:34
  22.8 2.2 reshape.150
  25.0 12.3 %all-to-all-start.1 = ((bf16[64,20,896]{2,1,0:T(8,128)(2,1)}), bf16[64,20,896]{2,1,0:T(8,128)(2,1)S(1)}, u32[]{:S(2)}, u32[]{:S(2)}) async-start(bf16[64,20,896]{2,1,0:T(8,128)(2,1)} %reshape.150), calls=%async_computation.1 | async-start | bytes 5505024 | tf_op jit(solution)/shard_map/all_to_all | solution.py:37
  37.3 16.1 %scatter_custom_fusion = bf16[1280,896]{1,0:T(8,128)(2,1)} fusion(s32[1024]{0:T(1024)S(1)} %bitcast.105, bf16[128,896]{1,0:T(8,128)(2,1)} %param.12, s32[1024]{0:T(1024)S(1)} %broadcast_clamp_fusion.1, bf16[]{:T(256)} %constant.14.clone.1), kind=kCustom, calls=%fused_computation.39 | custom fusion | bytes 2294272 | tf_op jit(solution)/shard_map/scatter | solution.py:35
  53.4 4.7 reshape.148
  58.1 44.4 %all-to-all-done.1 = bf16[64,20,896]{2,1,0:T(8,128)(2,1)S(1)} async-done(((bf16[64,20,896]{2,1,0:T(8,128)(2,1)}), bf16[64,20,896]{2,1,0:T(8,128)(2,1)S(1)}, u32[]{:S(2)}, u32[]{:S(2)}) %all-to-all-start.1) | async-done | bytes 2293792 | tf_op jit(solution)/shard_map/all_to_all | solution.py:37
  102.5 5.6 all-to-all-start
  110.2 4.1 convert_bitcast_fusion
  114.3 4.2 convert_bitcast_fusion.1
  118.5 54.9 %all-to-all-done = bf16[64,20,896]{2,1,0:T(8,128)(2,1)} async-done(((bf16[64,20,896]{2,1,0:T(8,128)(2,1)}), bf16[64,20,896]{2,1,0:T(8,128)(2,1)}, u32[]{:S(2)}, u32[]{:S(2)}) %all-to-all-start) | async-done | bytes 2293792 | tf_op jit(solution)/shard_map/all_to_all | solution.py:38
  173.4 2.3 copy.47
  176.3 4.2 convert_bitcast_fusion.2
  181.3 152.2 %all-reduce.8.cloned.1.call-done = (bf16[64,2,10,1024]{3,0,2,1:T(8,128)(2,1)}, bf16[64,2,10,1024]{3,0,2,1:T(8,128)(2,1)}, bf16[64,2,10,1024]{3,0,2,1:T(8,128)(2,1)}) async-done(((bf16[64,2,10,1024]{3,0,2,1:T(8,128)(2,1)}, bf16[64,2,10,1024]{3,0,2,1:T(8,128)(2,1)}, bf16[64,2,10,1024]{3,0,2,1:T(8,128)(2,1)}), (bf16[64,2,10,1024]{3,0,2,1:T(8,128)(2,1)}, bf16[64,2,10,1024]{3,0,2,1:T(8,128)(2,1)}, ...) | async-done | bytes 7864336 | tf_op jit(solution)/shard_map/psum | solution.py:49
  333.4 7.7 %fusion.11 = f32[2,64,10,896]{3,1,2,0:T(8,128)S(1)} fusion(bf16[2,896,1024]{2,1,0:T(8,128)(2,1)} %param.15, bf16[64,2,10,1024]{3,0,2,1:T(8,128)(2,1)} %get-tuple-element.12, bf16[64,2,10,1024]{3,0,2,1:T(8,128)(2,1)} %get-tuple-element.13, bf16[64,2,10,1024]{3,0,2,1:T(8,128)(2,1)} %get-tuple-element.14), kind=kOutput, calls=%fused_computation.22 | convolution fusion | flops 2365849600 | bytes 16121856 | tf_op jit(solution)/shard_map/sekh,edh->sekd/dot_general | solution.py:52
  341.1 3.4 add_convert_fusion
  344.5 2.9 copy.49
  347.4 10.8 %all-to-all-start.2 = ((bf16[64,20,896]{2,1,0:T(8,128)(2,1)}), bf16[64,20,896]{2,1,0:T(8,128)(2,1)}, u32[]{:S(2)}, u32[]{:S(2)}) async-start(bf16[64,20,896]{2,1,0:T(8,128)(2,1)} %copy.49), calls=%async_computation.2 | async-start | bytes 5505024 | tf_op jit(solution)/shard_map/all_to_all | solution.py:57
  358.8 6.9 %all-gather.2.cloned.1.call-done = bf16[1024,576]{0,1:T(8,128)(2,1)} async-done(((bf16[256,576]{0,1:T(8,128)(2,1)}), bf16[1024,576]{0,1:T(8,128)(2,1)}) %all-gather.2.cloned.1.call-update) | async-done | bytes 1179664 | tf_op jit(solution)/shard_map/all_gather | solution.py:71
  365.7 2.2 fusion.56
  369.9 2.1 fusion.21
  374.6 273.6 %all-reduce.6.cloned.1.call-done = f32[1024,576]{1,0:T(8,128)} async-done(((f32[1024,576]{1,0:T(8,128)}), f32[1024,576]{1,0:T(8,128)}) %all-reduce.6.cloned.1.call-update) | async-done | bytes 2359312
  649.6 3.5 reshape.153
  653.1 5.3 gather_fusion
  658.4 3.4 fusion.10
  (64 shorter events, 12.5 us)
Async XLA Ops:
  7.2 2.8 copy-start
  25.0 77.5 %all-to-all-start.1 = ((bf16[64,20,896]{2,1,0:T(8,128)(2,1)}), bf16[64,20,896]{2,1,0:T(8,128)(2,1)S(1)}, u32[]{:S(2)}, u32[]{:S(2)}) async-start(bf16[64,20,896]{2,1,0:T(8,128)(2,1)} %reshape.150), calls=%async_computation.1 | async-start | bytes 5505024 | tf_op jit(solution)/shard_map/all_to_all | solution.py:37
  102.5 70.9 %all-to-all-start = ((bf16[64,20,896]{2,1,0:T(8,128)(2,1)}), bf16[64,20,896]{2,1,0:T(8,128)(2,1)}, u32[]{:S(2)}, u32[]{:S(2)}) async-start(bf16[64,20,896]{2,1,0:T(8,128)(2,1)} %reshape.148), calls=%async_computation | async-start | bytes 5505024 | tf_op jit(solution)/shard_map/all_to_all | solution.py:38
  108.1 225.3 %all-reduce.8.cloned.1.call-start = ((), (), s32[]{:S(2)}) async-start(), calls=%async_computation.5 | async-start | bytes 15728640 | tf_op jit(solution)/shard_map/psum | solution.py:49
  108.1 2.0 copy-start.7
  110.2 4.1 copy-start.8
  173.4 2.9 copy-start.6
  180.5 185.2 %all-gather.2.cloned.1.call-start = ((), (), s32[]{:S(2)}) async-start(), calls=%async_computation.3 | async-start | bytes 1474560 | tf_op jit(solution)/shard_map/all_gather | solution.py:71
  333.4 7.7 %copy-start.9 = (bf16[2,896,1024]{2,1,0:T(8,128)(2,1)S(1)}, bf16[2,896,1024]{2,1,0:T(8,128)(2,1)}, u32[]{:S(2)}) copy-start(bf16[2,896,1024]{2,1,0:T(8,128)(2,1)} %param.16) | copy-start | bytes 11010052
  333.4 7.7 %copy-start.10 = (bf16[64,2,10,1024]{3,0,2,1:T(8,128)(2,1)S(1)}, bf16[64,2,10,1024]{3,0,2,1:T(8,128)(2,1)}, u32[]{:S(2)}) copy-start(bf16[64,2,10,1024]{3,0,2,1:T(8,128)(2,1)} %get-tuple-element.12) | copy-start | bytes 7864324
  333.4 7.7 %copy-start.11 = (bf16[64,2,10,1024]{3,0,2,1:T(8,128)(2,1)S(1)}, bf16[64,2,10,1024]{3,0,2,1:T(8,128)(2,1)}, u32[]{:S(2)}) copy-start(bf16[64,2,10,1024]{3,0,2,1:T(8,128)(2,1)} %get-tuple-element.13) | copy-start | bytes 7864324
  347.4 10.9 %copy-start.2 = (bf16[128,1152]{1,0:T(8,128)(2,1)S(1)}, bf16[128,1152]{1,0:T(8,128)(2,1)}, u32[]{:S(2)}) copy-start(bf16[128,1152]{1,0:T(8,128)(2,1)} %param.18) | copy-start | bytes 884740
  347.4 11.1 %copy-start.3 = (bf16[128,1024]{1,0:T(8,128)(2,1)S(1)}, bf16[128,1024]{1,0:T(8,128)(2,1)}, u32[]{:S(2)}) copy-start(bf16[128,1024]{1,0:T(8,128)(2,1)} %param.19) | copy-start | bytes 786436
  347.4 11.3 %copy-start.5 = (s32[128]{0:T(128)S(1)}, s32[128]{0:T(128)}, u32[]{:S(2)}) copy-start(s32[128]{0:T(128)} %param.20) | copy-start | bytes 1540
  347.4 302.2 %all-to-all-start.2 = ((bf16[64,20,896]{2,1,0:T(8,128)(2,1)}), bf16[64,20,896]{2,1,0:T(8,128)(2,1)}, u32[]{:S(2)}, u32[]{:S(2)}) async-start(bf16[64,20,896]{2,1,0:T(8,128)(2,1)} %copy.49), calls=%async_computation.2 | async-start | bytes 5505024 | tf_op jit(solution)/shard_map/all_to_all | solution.py:57
  358.2 290.0 %all-reduce.6.cloned.1.call-start = ((), (), s32[]{:S(2)}) async-start(), calls=%async_computation.4 | async-start | bytes 5242880
  368.0 1.3 copy-start.12
  372.0 0.7 copy-start.4
  372.0 1.3 copy-start.13
  653.1 8.6 %copy-start.1 = (bf16[128,896]{1,0:T(8,128)(2,1)S(1)}, bf16[128,896]{1,0:T(8,128)(2,1)}, u32[]{:S(2)}) copy-start(bf16[128,896]{1,0:T(8,128)(2,1)} %param.11) | copy-start | bytes 688132
Sparse Core Ops, SparseCore 0:
  180.6 152.7 all-reduce.7
  335.2 30.4 all-gather.1
  372.1 276.1 all-reduce.5
where the time goes:
time: 669 us; the launch traced here: 668 us
  waiting for transfers between devices  533 us (80%)
  local copies, waits for them, and re-layouts  58.4 us (9%)
  matrix products  29.3 us (4%)
  starting transfers between devices  29 us (4%)
  between operations  14 us (2%)
    unnamed x4, waiting for transfers between devices  274 us
    psum x1, waiting for transfers between devices, expert_layer(): lax.psum(down_part.astype(jnp.bfloat16), 'ctx').astype(jnp.float32)  152 us
    all_to_all x1, waiting for transfers between devices, expert_layer(): lax.all_to_all(send_grad, 'exp', split_axis=0, concat_axis=0, tiled=True)  54.9 us
    all_to_all x1, waiting for transfers between devices, expert_layer(): lax.all_to_all(send_input, 'exp', split_axis=0, concat_axis=0, tiled=True)  44.4 us
    scatter x1, local copies, waits for them, and re-layouts, expert_layer(): send_grad = empty.at[target].set(moe_grad[source_rows]).reshape(send_shape)  16.1 us
  transfers between devices with their start and end apart: 6, of which 5 were waited for; matrix products, arithmetic and copies ran while one was open for 8% of the time, Pallas kernels for 0%

commit v1 on v0

v1 whole, which is shorter than its diff:
```python
import jax
import jax.numpy as jnp
from jax import lax
from jax.experimental import pallas as pl
from jax.experimental.pallas import tpu as pltpu
from jax.sharding import PartitionSpec as P

SCORE_SCALE = 192.0 ** (-0.5)
MASKED = -1e30
MESH = pl.DeviceIdType.MESH
BF = jnp.bfloat16
F32 = jnp.float32

NX, NZ, NY, NC = 4, 8, 4, 2
NQ = NY * NC
TOK = 128
WID = 896
HID = 1024
CAP = 10
SLOTS = NZ * CAP
LAT = 576
VAL = 512
HEADS = 2
KEY_DEV = 256
KEYS = NX * KEY_DEV

N_ZAG = 16
N_META = 8
N_LAT = 4
N_PLANE = 32
N_BACK = 16
N_RS = 24
N_AG = 16
N_ZRS = 8
N_LG = 1 + 8 + 4 + 4

OFF_ZAG = 0
OFF_META = OFF_ZAG + N_ZAG
OFF_LAT = OFF_META + N_META
OFF_PLANE = OFF_LAT + N_LAT
OFF_BACK = OFF_PLANE + N_PLANE
OFF_RS = OFF_BACK + N_BACK
OFF_AG = OFF_RS + N_RS
OFF_ZRS = OFF_AG + N_AG
OFF_LG = OFF_ZRS + N_ZRS
N_SEM = OFF_LG + N_LG


def nn(a, b):
    return lax.dot_general(a, b, (((1,), (0,)), ((), ())), preferred_element_type=F32)


def nt(a, b):
    return lax.dot_general(a, b, (((1,), (1,)), ((), ())), preferred_element_type=F32)


def tn(a, b):
    return lax.dot_general(a, b, (((0,), (0,)), ((), ())), preferred_element_type=F32)


def body(
    in_hbm, grad_hbm, meta_hbm, wg_hbm, wu_hbm, wd_hbm, q_hbm, og_hbm, pos_ref, lat_hbm,
    out_ref, qg_ref, lg_ref,
    tok, meta, wg, wu, wd, qv, ogv, latraw, lat, rank_s, gate_s, pick, ysend, yrecv,
    part, rs_mid, rs_in, bk, rsend, rrecv, zsend_v, zhalf, zrecv,
    lacc, lout, lc_in, lz_out, lz_in, lx_out, lx_in, ly_out, ly_in,
    ssem, rsem, lsem,
):
    x = lax.axis_index("ctx")
    e_id = lax.axis_index("exp")
    z = e_id // NQ
    q = e_id % NQ
    y = q // NC
    c = q % NC

    def dev(xx, zz, qq):
        return (xx, zz * NQ + qq)

    def zdev(d):
        return dev(x, (z + d + NZ) % NZ, q)

    def xdev(d):
        return dev((x + d + NX) % NX, z, q)

    def plane(dy, dc):
        return ((y + dy + NY) % NY) * NC + (c + dc) % NC

    sends = []

    def copy(src, dst, idx, to):
        return pltpu.make_async_remote_copy(
            src_ref=src, dst_ref=dst, send_sem=ssem.at[idx], recv_sem=rsem.at[idx],
            device_id=to, device_id_type=MESH,
        )

    def send(src, dst, idx, to):
        op = copy(src, dst, idx, to)
        op.start()
        sends.append(op)

    def arrived(dst, idx, frm):
        copy(dst, dst, idx, frm).wait_recv()

    loads = []

    def load(src, dst):
        op = pltpu.make_async_copy(src, dst, lsem.at[len(loads)])
        op.start()
        loads.append(op)
        return op

    ld_in = load(in_hbm, tok.at[0, z])
    ld_meta = load(meta_hbm, meta.at[z])
    ld_lat = load(lat_hbm, latraw)
    ld_grad = load(grad_hbm, tok.at[1, z])
    ld_q = load(q_hbm, qv)
    ld_og = load(og_hbm, ogv)
    ld_wg = load(wg_hbm, wg)
    ld_wu = load(wu_hbm, wu)
    ld_wd = load(wd_hbm, wd)

    barrier = pltpu.get_barrier_semaphore()
    peers = [zdev(d) for d in range(1, NZ)]
    peers += [dev(x, z, plane(j // NC, j % NC)) for j in range(1, NQ)]
    peers += [xdev(d) for d in range(1, NX)]
    for peer in peers:
        pl.semaphore_signal(barrier, inc=1, device_id=peer, device_id_type=MESH)
    pl.semaphore_wait(barrier, len(peers))

    def zidx(a, way, step):
        return OFF_ZAG + (a * 2 + way) * 4 + step

    half = (pl.ds(0, TOK // 2), pl.ds(TOK // 2, TOK // 2))

    def zblock(a, way, step):
        b = (z - step + NZ) % NZ if way == 0 else (z + step) % NZ
        return tok.at[a, b] if step < 4 else tok.at[a, b, half[way]]

    def zsend(a, step):
        for way in (0, 1):
            b = (z - step + NZ) % NZ if way == 0 else (z + step) % NZ
            blk = tok.at[a, b] if step < 3 else tok.at[a, b, half[way]]
            send(blk, blk, zidx(a, way, step), zdev(1 if way == 0 else -1))

    def zarrive(a, step):
        for way in (0, 1):
            arrived(zblock(a, way, step), zidx(a, way, step - 1), zdev(-1 if way == 0 else 1))

    ld_in.wait()
    zsend(0, 0)
    ld_meta.wait()
    for d in range(1, NZ):
        send(meta.at[z], meta.at[z], OFF_META + d, zdev(d))

    ld_lat.wait()
    new = lax.broadcasted_iota(jnp.int32, (KEY_DEV, KEY_DEV), 0)
    old = lax.broadcasted_iota(jnp.int32, (KEY_DEV, KEY_DEV), 1)
    src = ((new // 16) % 8) * 32 + ((new // 4) % 4) * 8 + (new // 128) * 4 + new % 4
    shuffle = jnp.where(src == old, 1.0, 0.0).astype(BF)
    lat[x] = nn(shuffle, latraw[...]).astype(BF)
    for d in range(1, NX):
        send(lat.at[x], lat.at[x], OFF_LAT + d, xdev(d))

    for d in range(1, NZ):
        b = (z - d + NZ) % NZ
        arrived(meta.at[b], OFF_META + d, dev(x, b, q))
    tri = jnp.where(
        lax.broadcasted_iota(jnp.int32, (TOK, TOK), 0) < lax.broadcasted_iota(jnp.int32, (TOK, TOK), 1),
        1.0, 0.0,
    ).astype(BF)
    names = (lax.broadcasted_iota(jnp.int32, (2 * NQ, TOK), 0) + z * (2 * NQ)).astype(F32)
    for b in range(NZ):
        member = jnp.zeros((2 * NQ, TOK), F32)
        gate = jnp.zeros((2 * NQ, TOK), F32)
        for k in range(8):
            hit = meta[b, k : k + 1, :] == names
            member = jnp.where(hit, 1.0, member)
            gate = jnp.where(hit, meta[b, 8 + k : 9 + k, :], gate)
        rank = nn(member.astype(BF), tri)
        rank_s[b] = jnp.where(member > 0.0, rank, -1.0)
        gate_s[b] = gate

    def slot_value(b):
        row = lax.broadcasted_iota(jnp.int32, (SLOTS, TOK), 0)
        return jnp.where(row % NZ == b, row // NZ, -5).astype(F32)

    def build(weighted):
        for b in range(NZ):
            value = slot_value(b)

            def one(i, carry):
                row = rank_s[b, pl.ds(i, 1), :]
                if weighted:
                    cell = jnp.where(row == value, gate_s[b, pl.ds(i, 1), :], 0.0)
                else:
                    cell = jnp.where(row == value, 1.0, 0.0)
                pick[i, :, b * TOK : (b + 1) * TOK] = cell.astype(BF)
                return carry

            lax.fori_loop(0, 2 * NQ, one, 0)

    zarrive(0, 1)
    zsend(0, 1)

    ld_q.wait()
    ld_og.wait()
    for d in range(1, NX):
        arrived(lat.at[(x - d + NX) % NX], OFF_LAT + d, xdev(-d))

    col = lax.broadcasted_iota(jnp.int32, (TOK, KEYS), 1)
    key_pos = (
        (col // 256) * 256 + ((col // 16) % 8) * 32 + ((col // 4) % 4) * 8 + ((col // 128) % 2) * 4 + col % 4
    )

    def attention(h):
        keys = lat[...].reshape(KEYS, LAT)
        visible = key_pos <= pos_ref[...]
        qh = qv[h]
        gh = ogv[h]
        score = jnp.where(visible, nt(qh, keys) * SCORE_SCALE, MASKED)
        peak = jnp.max(score, axis=1, keepdims=True)
        raw = jnp.where(visible, jnp.exp(score - peak), 0.0)
        attend = raw / jnp.sum(raw, axis=1, keepdims=True)
        dots = nt(gh, keys[:, :VAL])
        row_dot = jnp.sum(attend * dots, axis=1, keepdims=True)
        grad = (attend * (dots - row_dot)).astype(BF)
        low = attend.astype(BF)
        qg_ref[h] = (nn(grad, keys) * SCORE_SCALE).astype(BF)
        key_part = tn(grad, qh) * SCORE_SCALE
        val_part = tn(low, gh)
        if h == 0:
            lacc[...] = key_part
        else:
            lacc[...] += key_part
        lacc[:, :VAL] += val_part

    attention(0)
    zarrive(0, 2)
    zsend(0, 2)
    attention(1)
    lout[...] = lacc[...].astype(BF).reshape(NX, NC, 128, LAT)
    sib = plane(0, 1)
    send(lout.at[:, 1 - c], lc_in, OFF_LG, dev(x, z, sib))
    zarrive(0, 3)
    zsend(0, 3)
    ld_grad.wait()
    zsend(1, 0)

    build(False)
    zarrive(0, 4)

    def pidx(a, e, j):
        return OFF_PLANE + (a * 2 + e) * NQ + j

    ORDER = (4, 5, 2, 3, 6, 7, 1)

    def pack(a):
        toks = tok[a].reshape(NZ * TOK, WID)

        def rows_for(qq):
            return nn(pick[pl.ds(qq * 2, 2)].reshape(2 * SLOTS, NZ * TOK), toks).astype(BF)

        for j in ORDER:
            qq = plane(j // NC, j % NC)
            ysend[a, qq] = rows_for(qq).reshape(2, SLOTS, WID)
            send(ysend.at[a, qq, 0], yrecv.at[a, 0, q], pidx(a, 0, j), dev(x, z, qq))
        own = rows_for(q).reshape(2, SLOTS, WID)
        yrecv[a, 0, q] = own[0]
        yrecv[a, 1, q] = own[1]
        for j in ORDER:
            qq = plane(j // NC, j % NC)
            send(ysend.at[a, qq, 1], yrecv.at[a, 1, q], pidx(a, 1, j), dev(x, z, qq))

    def rows_arrive(a, e):
        for j in range(1, NQ):
            frm = plane(-(j // NC), j % NC)
            arrived(yrecv.at[a, e, frm], pidx(a, e, j), dev(x, z, frm))

    pack(0)
    zarrive(1, 1)
    zsend(1, 1)

    arrived(lc_in, OFF_LG, dev(x, z, sib))
    mine = lacc[...].reshape(NX, NC, 128, LAT)
    summed = jnp.where(c == 0, mine[:, 0], mine[:, 1]) + lc_in[...].astype(F32)
    lacc[pl.ds(0, NX * 128)] = summed.reshape(NX * 128, LAT)
    lz_out[...] = summed.astype(BF).reshape(NX, NZ, 16, LAT)
    for d in range(1, NZ):
        send(lz_out.at[:, (z + d) % NZ], lz_in.at[d], OFF_LG + d, zdev(d))

    zarrive(1, 2)
    zsend(1, 2)

    ld_wg.wait()
    ld_wu.wait()
    ld_wd.wait()

    k_opp, k_right, k_left = (x + 2) % NX, (x + 1) % NX, (x + 3) % NX
    right, left = xdev(1), xdev(-1)
    top, bottom = pl.ds(0, SLOTS), pl.ds(SLOTS, SLOTS)

    def partial(e, name, k):
        a, w = {"gate": (0, wg), "up": (0, wu), "down": (1, wd)}[name]
        rows = yrecv[a, e, pl.ds(k * 2, 2)].reshape(2 * SLOTS, WID)
        return nt(rows, w[e]) if name == "down" else nn(rows, w[e])

    UNITS = ((0, 2, ("gate", "up")), (2, 1, ("down",)))

    def ridx(e, u, n):
        return OFF_RS + (e * 2 + u) * 6 + n

    def store_part(e, u, k):
        first, _, names_ = UNITS[u]
        for i, name in enumerate(names_):
            part[e, k, first + i] = partial(e, name, k).astype(BF)

    def reduce_first(e, u):
        first, n, _ = UNITS[u]
        rng = pl.ds(first, n)
        store_part(e, u, k_opp)
        send(part.at[e, k_opp, rng, top], rs_mid.at[0, e, rng], ridx(e, u, 0), right)
        send(part.at[e, k_opp, rng, bottom], rs_mid.at[1, e, rng], ridx(e, u, 1), left)
        store_part(e, u, k_right)
        send(part.at[e, k_right, rng, bottom], rs_in.at[0, e, rng, bottom], ridx(e, u, 2), right)
        store_part(e, u, k_left)
        send(part.at[e, k_left, rng, top], rs_in.at[1, e, rng, top], ridx(e, u, 3), left)

    def reduce_second(e, u):
        first, n, _ = UNITS[u]
        rng = pl.ds(first, n)
        arrived(rs_mid.at[0, e, rng], ridx(e, u, 0), left)
        got = rs_mid[0, e, rng].astype(F32) + part[e, k_right, rng, top].astype(F32)
        part[e, k_right, rng, top] = got.astype(BF)
        send(part.at[e, k_right, rng, top], rs_in.at[0, e, rng, top], ridx(e, u, 4), right)
        arrived(rs_mid.at[1, e, rng], ridx(e, u, 1), right)
        got = rs_mid[1, e, rng].astype(F32) + part[e, k_left, rng, bottom].astype(F32)
        part[e, k_left, rng, bottom] = got.astype(BF)
        send(part.at[e, k_left, rng, bottom], rs_in.at[1, e, rng, bottom], ridx(e, u, 5), left)
        store_part(e, u, x)

    def reduce_last(e):
        for u in (0, 1):
            first, n, _ = UNITS[u]
            rng = pl.ds(first, n)
            arrived(rs_in.at[0, e, rng, bottom], ridx(e, u, 2), left)
            arrived(rs_in.at[1, e, rng, top], ridx(e, u, 3), right)
            arrived(rs_in.at[0, e, rng, top], ridx(e, u, 4), left)
            arrived(rs_in.at[1, e, rng, bottom], ridx(e, u, 5), right)

    def total(e, i, rows):
        return (
            part[e, x, i, rows].astype(F32)
            + rs_in[0, e, i, rows].astype(F32)
            + rs_in[1, e, i, rows].astype(F32)
        )

    def aidx(e, way, n):
        return OFF_AG + (e * 2 + way) * 3 + n

    def swiglu_back(e):
        both = pl.ds(0, 2)
        for rows in (top, bottom):
            gate_pre, up_pre, hidden = (total(e, i, rows) for i in range(3))
            sigma = jax.nn.sigmoid(gate_pre)
            bk[e, x, 0, rows] = (hidden * up_pre * sigma * (1.0 + gate_pre * (1.0 - sigma))).astype(BF)
            bk[e, x, 1, rows] = (hidden * gate_pre * sigma).astype(BF)
        t, b = bk.at[e, x, both, top], bk.at[e, x, both, bottom]
        send(t, t, aidx(e, 0, 0), right)
        send(b, b, aidx(e, 1, 0), left)
        send(b, b, aidx(e, 0, 1), right)
        send(t, t, aidx(e, 1, 1), left)

    def gather_forward(e):
        both = pl.ds(0, 2)
        t = bk.at[e, k_left, both, top]
        arrived(t, aidx(e, 0, 0), left)
        send(t, t, aidx(e, 0, 2), right)
        b = bk.at[e, k_right, both, bottom]
        arrived(b, aidx(e, 1, 0), right)
        send(b, b, aidx(e, 1, 2), left)

    def gather_near(e):
        both = pl.ds(0, 2)
        arrived(bk.at[e, k_left, both, bottom], aidx(e, 0, 1), left)
        arrived(bk.at[e, k_right, both, top], aidx(e, 1, 1), right)

    def gather_far(e):
        both = pl.ds(0, 2)
        arrived(bk.at[e, k_opp, both, top], aidx(e, 0, 2), left)
        arrived(bk.at[e, k_opp, both, bottom], aidx(e, 1, 2), right)

    def bidx(e, j):
        return OFF_BACK + e * NQ + j

    def route(e, k):
        rows = nt(bk[e, k, 0], wg[e]) + nt(bk[e, k, 1], wu[e])
        rsend[e, pl.ds(k * 2, 2)] = rows.astype(BF).reshape(2, SLOTS, WID)
        for cc in range(NC):
            qq = k * NC + cc
            j = ((k - y + NY) % NY) * NC + (cc + c) % NC

            @pl.when(j != 0)
            def _():
                copy(rsend.at[e, qq], rrecv.at[q, e], bidx(e, j), dev(x, z, qq)).start()

            @pl.when(j == 0)
            def _():
                rrecv[q, e] = rsend[e, qq]

    rows_arrive(0, 0)
    reduce_first(0, 0)
    zarrive(1, 3)
    zsend(1, 3)
    reduce_second(0, 0)
    zarrive(1, 4)
    pack(1)
    rows_arrive(0, 1)
    reduce_first(1, 0)
    reduce_second(1, 0)
    build(True)

    zsum = lacc[pl.ds(0, NX * 128)].reshape(NX, NZ, 16, LAT)
    zown = jnp.where(z == 0, zsum[:, 0], 0.0)
    for b in range(1, NZ):
        zown = zown + jnp.where(z == b, zsum[:, b], 0.0)
    for d in range(1, NZ):
        arrived(lz_in.at[d], OFF_LG + d, zdev(-d))
        zown = zown + lz_in[d].astype(F32)
    lx_out[...] = zown
    for d in range(1, NX):
        send(lx_out.at[(x + d) % NX], lx_in.at[d], OFF_LG + 8 + d, xdev(d))

    rows_arrive(1, 0)
    reduce_first(0, 1)
    reduce_second(0, 1)
    rows_arrive(1, 1)
    reduce_first(1, 1)
    reduce_last(0)
    swiglu_back(0)
    reduce_second(1, 1)

    xsum = lx_out[x]
    for d in range(1, NX):
        arrived(lx_in.at[d], OFF_LG + 8 + d, xdev(-d))
        xsum = xsum + lx_in[d]
    ly_out[...] = xsum
    for d in range(1, NY):
        send(ly_out, ly_in.at[d], OFF_LG + 12 + d, dev(x, z, plane(d, 0)))

    gather_forward(0)
    route(0, x)
    reduce_last(1)
    swiglu_back(1)
    gather_near(0)
    route(0, k_left)
    route(0, k_right)
    gather_far(0)
    route(0, k_opp)
    gather_forward(1)
    route(1, x)
    gather_near(1)
    route(1, k_left)
    route(1, k_right)

    ysum = ly_out[...]
    for d in range(1, NY):
        arrived(ly_in.at[d], OFF_LG + 12 + d, dev(x, z, plane(-d, 0)))
        ysum = ysum + ly_in[d]
    pick4 = jnp.where(y == 0, ysum[0:4], 0.0)
    for b in range(1, NY):
        pick4 = pick4 + jnp.where(y == b, ysum[4 * b : 4 * b + 4], 0.0)
    lg_ref[...] = pick4

    gather_far(1)
    route(1, k_opp)

    for e in (0, 1):
        for j in range(1, NQ):
            frm = plane(-(j // NC), j % NC)
            arrived(rrecv.at[frm, e], bidx(e, j), dev(x, z, frm))

    def tokens(b):
        cols = pl.ds(pl.multiple_of(b * TOK, TOK), TOK)
        return tn(
            pick[:, :, cols].reshape(2 * NQ * SLOTS, TOK), rrecv[...].reshape(2 * NQ * SLOTS, WID)
        )

    def widx(way, step):
        return OFF_ZRS + way * 4 + step

    far = tokens((z + 4) % NZ).astype(BF)
    zhalf[0] = far[: TOK // 2]
    zhalf[1] = far[TOK // 2 :]
    for way in (0, 1):
        to = zdev(1 if way == 0 else -1)
        send(zhalf.at[way], zrecv.at[way, 0, half[way]], widx(way, 0), to)
    for step in (1, 2, 3):
        for way in (0, 1):
            b = (z + 4 - step) % NZ if way == 0 else (z + 4 + step) % NZ
            to = zdev(1 if way == 0 else -1)
            frm = zdev(-1 if way == 0 else 1)
            acc = tokens(b)
            if step == 1:
                arrived(zrecv.at[way, 0, half[way]], widx(way, 0), frm)
                got = zrecv[way, 0, half[way]].astype(F32)
                lo, hi = acc[: TOK // 2], acc[TOK // 2 :]
                if way == 0:
                    lo = lo + got
                else:
                    hi = hi + got
                acc = jnp.concatenate([lo, hi], axis=0)
            else:
                arrived(zrecv.at[way, step - 1], widx(way, step - 1), frm)
                acc = acc + zrecv[way, step - 1].astype(F32)
            zsend_v[way, step - 1] = acc.astype(BF)
            send(zsend_v.at[way, step - 1], zrecv.at[way, step], widx(way, step), to)
    final = tokens(z)
    for way in (0, 1):
        frm = zdev(-1 if way == 0 else 1)
        arrived(zrecv.at[way, 3], widx(way, 3), frm)
        final = final + zrecv[way, 3].astype(F32)
    out_ref[...] = final.astype(BF)

    for op in sends:
        op.wait_send()
    for e in (0, 1):
        for j in range(1, NQ):
            copy(rsend.at[e, 0], rrecv.at[0, e], bidx(e, j), dev(x, z, plane(j // NC, j % NC))).wait_send()


def per_device(
    moe_input, moe_grad, routes, gates, w_gate, w_up, w_down, queries, out_grad, positions, latents
):
    meta = jnp.concatenate([routes.T.astype(F32), gates.T], axis=0)
    q_heads = queries.reshape(TOK, HEADS, LAT).transpose(1, 0, 2)
    g_heads = out_grad.reshape(TOK, HEADS, VAL).transpose(1, 0, 2)
    anywhere = pl.BlockSpec(memory_space=pl.ANY)
    vmem = pl.BlockSpec(memory_space=pltpu.VMEM)
    scratch = [
        pltpu.VMEM((2, NZ, TOK, WID), BF),
        pltpu.VMEM((NZ, 16, TOK), F32),
        pltpu.VMEM((2, WID, HID), BF),
        pltpu.VMEM((2, WID, HID), BF),
        pltpu.VMEM((2, HID, WID), BF),
        pltpu.VMEM((HEADS, TOK, LAT), BF),
        pltpu.VMEM((HEADS, TOK, VAL), BF),
        pltpu.VMEM((KEY_DEV, LAT), BF),
        pltpu.VMEM((NX, KEY_DEV, LAT), BF),
        pltpu.VMEM((NZ, 2 * NQ, TOK), F32),
        pltpu.VMEM((NZ, 2 * NQ, TOK), F32),
        pltpu.VMEM((2 * NQ, SLOTS, NZ * TOK), BF),
        pltpu.VMEM((2, NQ, 2, SLOTS, WID), BF),
        pltpu.VMEM((2, 2, NQ, SLOTS, WID), BF),
        pltpu.VMEM((2, NX, 3, 2 * SLOTS, HID), BF),
        pltpu.VMEM((2, 2, 3, SLOTS, HID), BF),
        pltpu.VMEM((2, 2, 3, 2 * SLOTS, HID), BF),
        pltpu.VMEM((2, NX, 2, 2 * SLOTS, HID), BF),
        pltpu.VMEM((2, NQ, SLOTS, WID), BF),
        pltpu.VMEM((NQ, 2, SLOTS, WID), BF),
        pltpu.VMEM((2, 3, TOK, WID), BF),
        pltpu.VMEM((2, TOK // 2, WID), BF),
        pltpu.VMEM((2, 4, TOK, WID), BF),
        pltpu.VMEM((KEYS, LAT), F32),
        pltpu.VMEM((NX, NC, 128, LAT), BF),
        pltpu.VMEM((NX, 128, LAT), BF),
        pltpu.VMEM((NX, NZ, 16, LAT), BF),
        pltpu.VMEM((NZ, NX, 16, LAT), BF),
        pltpu.VMEM((NX, 16, LAT), F32),
        pltpu.VMEM((NX, 16, LAT), F32),
        pltpu.VMEM((16, LAT), F32),
        pltpu.VMEM((NY, 16, LAT), F32),
        pltpu.SemaphoreType.DMA((N_SEM,)),
        pltpu.SemaphoreType.DMA((N_SEM,)),
        pltpu.SemaphoreType.DMA((9,)),
    ]
    out, q_grad, lat_grad = pl.pallas_call(
        body,
        out_shape=(
            jax.ShapeDtypeStruct((TOK, WID), BF),
            jax.ShapeDtypeStruct((HEADS, TOK, LAT), BF),
            jax.ShapeDtypeStruct((4, LAT), F32),
        ),
        in_specs=[anywhere] * 8 + [vmem] + [anywhere],
        out_specs=(vmem, vmem, vmem),
        scratch_shapes=scratch,
        compiler_params=pltpu.CompilerParams(
            collective_id=0, has_side_effects=True, vmem_limit_bytes=63 * 2**20
        ),
    )(
        moe_input, moe_grad, meta, w_gate, w_up, w_down, q_heads, g_heads,
        positions.reshape(TOK, 1), latents,
    )
    return (out, q_grad.transpose(1, 0, 2).reshape(TOK, HEADS * LAT), lat_grad)


def solution(mesh):
    return jax.shard_map(
        per_device,
        mesh=mesh,
        in_specs=(
            P("exp", "ctx"),
            P("exp", "ctx"),
            P("exp", None),
            P("exp", None),
            P("exp", "ctx", None),
            P("exp", "ctx", None),
            P("exp", None, "ctx"),
            P("ctx", "exp"),
            P("ctx", "exp"),
            P("ctx"),
            P("ctx", None),
        ),
        out_specs=(P("exp", "ctx"), P("ctx", "exp"), P(("ctx", "exp"), None)),
        check_vma=False,
    )
```

time: 669 us -> 225 us (0.34)
  waiting for transfers between devices: 533 us -> 0 us
  Pallas kernels: 0 us -> 210 us
  local copies, waits for them, and re-layouts: 58.4 us -> 12.3 us
  matrix products: 29.3 us -> 0 us
  starting transfers between devices: 29 us -> 0 us
  between operations: 14 us -> 0.65 us
    unnamed x4 -> x0, waiting for transfers between devices: 274 us -> none
    pallas_call x0 -> x1, Pallas kernels: none -> 210 us  [per_device(): pl.pallas_call(body, out_shape=(jax.ShapeDtypeStruct((TOK, WID), BF), jax...]
    psum x1 -> x0, waiting for transfers between devices: 152 us -> none  [expert_layer(): lax.psum(down_part.astype(jnp.bfloat16), 'ctx').astype(jnp.float32)]
    all_to_all x3 -> x0, waiting for transfers between devices: 99.3 us -> none  [the longest x1 54.9 us: expert_layer(): lax.all_to_all(send_grad, 'exp', split_axis=0, concat_axis=0, tiled=True)]
    scatter x2 -> x0, local copies, waits for them, and re-layouts: 28.9 us -> none  [the longest x1 16.1 us: expert_layer(): send_grad = empty.at[target].set(moe_grad[source_rows]).reshape(send_shape)]
    all_to_all x3 -> x0, starting transfers between devices: 28.7 us -> none  [the longest x1 12.3 us: expert_layer(): lax.all_to_all(send_input, 'exp', split_axis=0, concat_axis=0, tiled=True)]
    dot_general x9 -> x0, matrix products: 27.1 us -> none  [the longest x1 7.67 us: expert_layer(): jnp.einsum('sekh,edh->sekd', gate_back, w_gate, preferred_element_type=jn...]
    reshape x5 -> x3, local copies, waits for them, and re-layouts: 13.4 us -> 3.14 us  [the longest x1 1.39 us: per_device(): positions.reshape(TOK, 1)]
  transfers between devices with their start and end apart: 6 -> 0, of which waited for: 5 -> 0; matrix products, arithmetic and copies ran while one was open for 8% -> 0% of each run, Pallas kernels for 0% -> 0%
where the time goes in v1:
time: 225 us
  Pallas kernels  210 us (93%)
  local copies, waits for them, and re-layouts  12.3 us (5%)
    pallas_call x1, Pallas kernels, per_device(): pl.pallas_call(body, out_shape=(jax.ShapeDtypeStruct((TOK, WID), BF), jax...  210 us
    unnamed x6, local copies, waits for them, and re-layouts  7.99 us

profile of v1, /device:TPU:4, one launch (start us, length us, event | category | flops | bytes accessed | tf_op | source)
XLA Modules:
  0.0 225.0 jit_solution(14382120099837193520)
XLA Ops:
  0.6 0.7 convert_bitcast_fusion
  1.3 1.3 pad_maximum_fusion.meta_hbm
  2.6 1.4 copy.20.pos_ref
  4.0 1.1 copy.18
  5.1 0.9 copy.19
  6.0 1.2 copy.16
  7.1 0.9 copy.17
  8.0 1.9 copy.21.lat_hbm
  9.9 210.0 %shard_map.130 = (bf16[128,896]{1,0:T(8,128)(2,1)}, bf16[2,128,576]{2,1,0:T(8,128)(2,1)}, f32[4,576]{1,0:T(4,128)}) custom-call(bf16[128,896]{1,0:T(8,128)(2,1)} %in_hbm.1, bf16[128,896]{1,0:T(8,128)(2,1)} %grad_hbm.1, f32[16,128]{1,0:T(8,128)} %pad_maximum_fusion.meta_hbm, bf16[2,896,1024]{2,1,0:T(8,128)(2,1)} %wg_hbm.1, bf16[2,896,1024]{2,1,0:T(8,128)(2,1)} %wu_hbm.1, ...), custom_call_target="tpu_custom_call" | custom-call | tf_op jit(solution)/shard_map/pallas_call | solution.py:576
  220.0 1.2 copy.22
  221.1 0.9 copy.23
  222.0 1.6 copy.26
  223.7 1.3 copy.27
